TPU v7x, 32 devices: a whole 2x2x4 slice. The times are simulated.
32 devices in a mesh: req: 8 (over z, x), mlp: 4 (over y, core).
Axes of the slice: x: 2, y: 2, z: 4, core: 2. Of those that a mesh axis runs over, the one named last changes fastest.
Arguments:
- tokens: bfloat16 [4096, 4096], P('req'), may hold values from -16 to 16
- grid_sides: int32 [16, 2], P('req'), may hold values from 10 to 14, as said below
- offsets: int32 [16], P('req'), may hold values from 0 to 201, as said below
- merge_rows: int32 [1024, 4], P('req'), may hold values from 0 to 401, as said below
- routes: int32 [1024, 1], replicated, may hold values from 0 to 7; in each aligned block of 128 rows (0 to 127, 128 to 255, ...) at most 16 rows name the same one
- norm_gain: float32 [2, 4096], replicated, may hold values from 0.5 to 1.5
- norm_bias: float32 [2, 4096], replicated, may hold values from -1.5 to 1.5
- layer_scale: float32 [2, 4096], replicated, may hold values from 0.2 to 1
- qkv_weight: bfloat16 [4096, 6144], P('req', 'mlp'), may hold values from -2.34375 to 2.34375
- out_weight: bfloat16 [2048, 4096], P('mlp', 'req'), may hold values from -0.125 to 0.125
- gate_up: bfloat16 [2, 4096, 4096], P(None, 'req', 'mlp'), may hold values from -0.09375 to 0.09375
- down_weight: bfloat16 [4096, 4096], P('mlp', 'req'), may hold values from -0.09375 to 0.09375
- merge_gain: float32 [4, 4096], P(None, 'mlp'), may hold values from 0.5 to 1.5
- merge_bias: float32 [4, 4096], P(None, 'mlp'), may hold values from -1.5 to 1.5
- merge_weight: bfloat16 [4, 4096, 2048], P(None, 'mlp', 'req'), may hold values from -0.1875 to 0.1875
Outputs:
- embeds: bfloat16 [1024, 2048], P('req', 'mlp')
- token_norms: float32 [1024], P('req')
- max_logits: float32 [16, 16], P('req', 'mlp')
Inputs may be any that keep to these rules, and one draw needn't show every extreme that they name: `grid_sides`: sides are even; the first 2 of all 16 images are 14 x 14 and the last image is 10 x 10. `offsets`: the images of a group are packed in order from in-group row 0: image g * 2 + j starts at the sum of 5 + h w over images g * 2 to g * 2 + j - 1. `merge_rows`: for slot k of group g, image i = g * 2 + k div 64 of grid h x w at offset o and m = k mod 64: if m < (h / 2)(w / 2), the entries are o + 5 + (2 a + e) w + 2 b + f for (e, f) = (0, 0), (0, 1), (1, 0), (1, 1), with a = m div (w / 2), b = m mod (w / 2); otherwise all four are 0. `routes`: among the 128 slots of one group, no value appears more than 16 times.
All inputs are finite; a program needn't handle non-finite values.
Results may differ from a plain program's by a relative error of at most 0.017.
Values may be sent and summed in bfloat16 or wider, within the bound.
A program may use at most 128 MiB of HBM per device.

v0:
```python
import math
import jax
import jax.numpy as jnp
from jax import lax
from jax.sharding import PartitionSpec as P

HEAD = 128
OUT = 2048
MSLOT = 64
CAP = 16
EPS = 1e-06


def layer_norm(values, scale_vec, shift_vec):
    center = jnp.mean(values, axis=-1, keepdims=True)
    offset_vals = values - center
    spread = jnp.mean(offset_vals * offset_vals, axis=-1, keepdims=True)
    return offset_vals * lax.rsqrt(spread + EPS) * scale_vec + shift_vec


def row_layout(grid_part, starts, row_count, head_size):
    position = jnp.arange(row_count, dtype=jnp.int32)
    lengths = 5 + grid_part[:, 0] * grid_part[:, 1]
    inside = (
        (position[:, None] >= starts[None, :]) & (position[:, None] < (starts + lengths)[None, :])
    ).astype(jnp.int32)
    present = jnp.sum(inside, axis=1)
    numbers = jnp.arange(grid_part.shape[0], dtype=jnp.int32)
    image_id = jnp.sum(inside * numbers[None, :], axis=1) + present - 1
    local_row = position - jnp.sum(inside * starts[None, :], axis=1)
    height = jnp.sum(inside * grid_part[None, :, 0], axis=1) + 1 - present
    breadth = jnp.sum(inside * grid_part[None, :, 1], axis=1) + 1 - present
    is_patch = (local_row >= 5) & (present > 0)
    patch_idx = jnp.maximum(local_row - 5, 0)
    coord_y = jnp.where(
        is_patch,
        (2.0 * (patch_idx // breadth).astype(jnp.float32) + 1.0) / height.astype(jnp.float32) - 1.0,
        0.0,
    )
    coord_x = jnp.where(
        is_patch,
        (2.0 * (patch_idx % breadth).astype(jnp.float32) + 1.0) / breadth.astype(jnp.float32) - 1.0,
        0.0,
    )
    quarter = head_size // 4
    frequency = math.pi * 100.0 ** (-jnp.arange(quarter, dtype=jnp.float32) / quarter)
    angle_y = (coord_y[:, None] * frequency[None, :])[:, None, :]
    angle_x = (coord_x[:, None] * frequency[None, :])[:, None, :]
    return (image_id, (jnp.cos(angle_y), jnp.sin(angle_y), jnp.cos(angle_x), jnp.sin(angle_x)))


def rotate(vectors, tables):
    cos_y, sin_y, cos_x, sin_x = tables
    quarter = vectors.shape[-1] // 4
    upper_y = vectors[..., :quarter]
    lower_y = vectors[..., quarter : 2 * quarter]
    upper_x = vectors[..., 2 * quarter : 3 * quarter]
    lower_x = vectors[..., 3 * quarter :]
    return jnp.concatenate(
        [
            upper_y * cos_y - lower_y * sin_y,
            upper_y * sin_y + lower_y * cos_y,
            upper_x * cos_x - lower_x * sin_x,
            upper_x * sin_x + lower_x * cos_x,
        ],
        axis=-1,
    )


def attend(queries, key_rows, values, image_id, numbers):
    scores = jnp.einsum(
        "qhd,khd->hqk", queries, key_rows, preferred_element_type=jnp.float32
    ) / math.sqrt(queries.shape[-1])
    same_image = image_id[:, None] == image_id[None, :]
    scores = jnp.where(same_image[None], scores, -jnp.inf)
    row_peak = jnp.max(scores, axis=-1)
    expo_vals = jnp.exp(scores - row_peak[..., None])
    weights = (expo_vals / jnp.sum(expo_vals, axis=-1, keepdims=True)).astype(jnp.bfloat16)
    attended = jnp.einsum(
        "hqk,khd->qhd", weights, values, preferred_element_type=jnp.float32
    ).astype(jnp.bfloat16)
    owned = image_id[None, None, :] == numbers[:, None, None]
    logits = jnp.max(jnp.where(owned, row_peak[None], -jnp.inf), axis=-1)
    return (attended, logits)


def on_device(
    tokens,
    grid_sides,
    offsets,
    merge_rows,
    routes,
    norm_gain,
    norm_bias,
    layer_scale,
    qkv_weight,
    out_weight,
    gate_up,
    down_weight,
    merge_gain,
    merge_bias,
    merge_weight,
):
    row_count = tokens.shape[0]
    model_width = tokens.shape[1]
    groups = lax.axis_size("req")
    shards = lax.axis_size("mlp")
    group_id = lax.axis_index("req")
    member = lax.axis_index("mlp")
    piece_width = model_width // shards
    start_col = member * piece_width
    slot_count = merge_rows.shape[0]
    numbers = jnp.arange(grid_sides.shape[0], dtype=jnp.int32)
    image_id, tables = row_layout(grid_sides, offsets, row_count, HEAD)
    normed = layer_norm(tokens.astype(jnp.float32), norm_gain[0], norm_bias[0]).astype(jnp.bfloat16)
    columns = normed
    mixed_qkv = jnp.dot(
        columns,
        lax.all_gather(qkv_weight, "req", axis=0, tiled=True),
        preferred_element_type=jnp.float32,
    )
    heads_here = qkv_weight.shape[1] // (3 * HEAD)
    mixed_qkv = mixed_qkv.reshape(row_count, heads_here, 3, HEAD)
    queries = rotate(mixed_qkv[:, :, 0], tables).astype(jnp.bfloat16)
    key_rows = rotate(mixed_qkv[:, :, 1], tables).astype(jnp.bfloat16)
    values = mixed_qkv[:, :, 2].astype(jnp.bfloat16)
    attended, logits = attend(queries, key_rows, values, image_id, numbers)
    attended_flat = attended.reshape(row_count, heads_here * HEAD)
    head_terms = jnp.dot(
        attended_flat,
        lax.all_gather(out_weight, "req", axis=1, tiled=True),
        preferred_element_type=jnp.float32,
    )
    attn_sum = lax.psum(head_terms.astype(jnp.bfloat16), "mlp").astype(jnp.float32)
    residual = (tokens.astype(jnp.float32) + layer_scale[0] * attn_sum).astype(jnp.bfloat16)
    resid_piece = lax.dynamic_slice_in_dim(residual, start_col, piece_width, 1)
    normed_two = layer_norm(residual.astype(jnp.float32), norm_gain[1], norm_bias[1]).astype(
        jnp.bfloat16
    )
    columns = normed_two
    gate_pair = jnp.einsum(
        "rk,pkn->prn",
        columns,
        lax.all_gather(gate_up, "req", axis=1, tiled=True),
        preferred_element_type=jnp.float32,
    )
    hidden = (jax.nn.silu(gate_pair[0]) * gate_pair[1]).astype(jnp.bfloat16)
    hidden_terms = jnp.dot(
        hidden,
        lax.all_gather(down_weight, "req", axis=1, tiled=True),
        preferred_element_type=jnp.float32,
    )
    ffn_piece = lax.psum_scatter(
        hidden_terms.astype(jnp.bfloat16), "mlp", scatter_dimension=1, tiled=True
    ).astype(jnp.float32)
    own_scale_two = lax.dynamic_slice_in_dim(layer_scale[1], start_col, piece_width, 0)
    final_piece = (resid_piece.astype(jnp.float32) + own_scale_two * ffn_piece).astype(jnp.bfloat16)
    merged = final_piece[merge_rows].astype(jnp.float32)
    totals, squares = lax.psum(
        (jnp.sum(merged, axis=(1, 2)), jnp.sum(merged * merged, axis=(1, 2))), "mlp"
    )
    center = totals / (4 * model_width)
    spread = squares / (4 * model_width) - center * center
    scaled = (
        (merged - center[:, None, None]) * lax.rsqrt(spread + EPS)[:, None, None] * merge_gain[None]
        + merge_bias[None]
    ).astype(jnp.bfloat16)
    scaled_flat = scaled.reshape(slot_count, 4 * piece_width)
    piece_rows = lax.all_gather(merge_weight, "req", axis=2, tiled=True)
    merge_terms = jnp.dot(
        scaled_flat,
        piece_rows.reshape(4 * piece_width, piece_rows.shape[2]),
        preferred_element_type=jnp.float32,
    )
    projected = lax.psum_scatter(
        merge_terms.astype(jnp.bfloat16), "mlp", scatter_dimension=1, tiled=True
    ).astype(jnp.float32)
    slot_ids = jnp.arange(slot_count, dtype=jnp.int32)
    owner_grid = grid_sides[slot_ids // MSLOT]
    is_live = slot_ids % MSLOT < owner_grid[:, 0] // 2 * (owner_grid[:, 1] // 2)
    projected = jnp.where(is_live[:, None], projected, 0.0).astype(jnp.bfloat16)
    out_cols = projected.shape[1]
    own_routes = lax.dynamic_slice_in_dim(routes, group_id * slot_count, slot_count, 0)[:, 0]
    onehot = (own_routes[:, None] == jnp.arange(groups, dtype=jnp.int32)[None, :]).astype(jnp.int32)
    before = jnp.cumsum(onehot, axis=0) - onehot
    ranks = jnp.sum(before * onehot, axis=1)
    send_rows = (
        jnp.zeros((groups * CAP, out_cols), jnp.bfloat16)
        .at[own_routes * CAP + ranks]
        .set(projected)
    )
    received = lax.all_to_all(
        send_rows.reshape(groups, CAP, out_cols), "req", split_axis=0, concat_axis=0, tiled=True
    )
    embeds = received.reshape(groups * CAP, out_cols)
    row_squares = jnp.sum(jnp.square(embeds.astype(jnp.float32)), axis=1)
    total_squares = lax.psum(row_squares, "mlp")
    token_norms = jnp.sqrt(total_squares / OUT + EPS)
    return (embeds, token_norms, logits)


def solution(mesh):
    placed = (
        P("req", None),
        P("req", None),
        P("req"),
        P("req", None),
        P(),
        P(),
        P(),
        P(),
        P("req", "mlp"),
        P("mlp", "req"),
        P(None, "req", "mlp"),
        P("mlp", "req"),
        P(None, "mlp"),
        P(None, "mlp"),
        P(None, "mlp", "req"),
    )
    return jax.shard_map(
        on_device,
        mesh=mesh,
        in_specs=placed,
        out_specs=(P("req", "mlp"), P("req"), P("req", "mlp")),
        check_vma=False,
    )
```

profile of v0, /device:TPU:0, one launch (start us, length us, event | category | flops | bytes accessed | tf_op | source)
XLA Modules:
  0.0 1053.9 jit_solution(7051907031724275753)
XLA Ops:
  7.2 0.7 all-gather.6.cloned.1.call-update
  8.0 0.7 all-gather.8.cloned.1.call-update
  8.7 1.1 slice_reduce_fusion
  9.8 0.9 add_add_fusion.1
  10.7 0.8 select_reduce_fusion.5
  11.5 2.8 convert_reduce_fusion
  14.3 1.2 fusion.4
  15.9 3.0 multiply_cosine_fusion.1
  19.0 170.4 %all-gather.6.cloned.1.call-done = bf16[4096,1536]{1,0:T(8,128)(2,1)} async-done(((bf16[512,1536]{1,0:T(8,128)(2,1)}), bf16[4096,1536]{1,0:T(8,128)(2,1)}) %all-gather.6.cloned.1.call-update) | async-done | bytes 12582928 | tf_op jit(solution)/shard_map/all_gather | solution.py:119
  189.4 11.7 %fusion.16 = f32[512,1536]{0,1:T(8,128)S(1)} fusion(bf16[4096,1536]{1,0:T(8,128)(2,1)} %all-gather.6.cloned.1.call-done, bf16[512,4096]{1,0:T(8,128)(2,1)} %param.15, f32[4096]{0:T(1024)S(1)} %bitcast.60, f32[4096]{0:T(1024)S(1)} %bitcast.59, f32[512]{0:T(512)S(1)} %add_rsqrt_fusion.1, f32[512]{0:T(512)S(1)} %broadcast_multiply_fusion.1), kind=kOutput, calls=%fused_computation.25 | convolution fusion | flops 6455033856 | bytes 19959808 | tf_op jit(solution)/shard_map/dot_general | solution.py:117
  201.2 1.5 copy-done.8
  202.7 0.3 copy.46
  203.0 0.3 copy.47
  203.4 2.2 subtract_convert_fusion.3
  205.6 0.9 subtract_convert_fusion.1
  206.5 2.1 fusion.26
  208.6 0.9 fusion.27
  209.5 2.7 fusion.39
  212.2 52.4 %all-gather.8.cloned.1.call-done = bf16[512,4096]{1,0:T(8,128)(2,1)} async-done(((bf16[512,512]{1,0:T(8,128)(2,1)}), bf16[512,4096]{1,0:T(8,128)(2,1)}) %all-gather.8.cloned.1.call-update) | async-done | bytes 4194320 | tf_op jit(solution)/shard_map/all_gather | solution.py:131
  264.6 6.5 convolution_convert_fusion.1
  271.2 0.5 all-gather.10.cloned.1.call-update
  271.8 0.5 all-gather.12.cloned.1.call-update
  272.7 82.3 %all-reduce.3.cloned.1.call-done = bf16[512,4096]{1,0:T(8,128)(2,1)} async-done(((bf16[512,4096]{1,0:T(8,128)(2,1)}), bf16[512,4096]{1,0:T(8,128)(2,1)}) %all-reduce.3.cloned.1.call-update) | async-done | bytes 4194320 | tf_op jit(solution)/shard_map/psum | solution.py:134
  355.0 5.6 convert_reduce_fusion.1
  360.6 1.9 copy-done.3
  362.5 1.2 fusion.8
  363.7 221.3 %all-gather.10.cloned.1.call-done = bf16[2,4096,1024]{2,1,0:T(8,128)(2,1)} async-done(((bf16[2,512,1024]{2,1,0:T(8,128)(2,1)}), bf16[2,4096,1024]{2,1,0:T(8,128)(2,1)}) %all-gather.10.cloned.1.call-update) | async-done | bytes 16777232 | tf_op jit(solution)/shard_map/all_gather | solution.py:144
  585.1 15.0 %fusion.29 = f32[2,512,1024]{2,1,0:T(8,128)} fusion(bf16[2,4096,1024]{2,1,0:T(8,128)(2,1)} %all-gather.10.cloned.1.call-done, bf16[512,4096]{1,0:T(8,128)(2,1)} %copy-done.3, f32[4096]{0:T(1024)S(1)} %bitcast.58, f32[4096]{0:T(1024)S(1)} %bitcast.57, f32[512]{0:T(512)S(1)} %add_rsqrt_fusion, f32[512]{0:T(512)S(1)} %broadcast_multiply_fusion), kind=kOutput, calls=%fused_computation.41 | convolution fusion | flops 8602517504 | bytes 25202688 | tf_op jit(solution)/shard_map/rk,pkn->prn/dot_general | solution.py:141
  600.1 110.7 %all-gather.12.cloned.1.call-done = bf16[1024,4096]{1,0:T(8,128)(2,1)} async-done(((bf16[1024,512]{1,0:T(8,128)(2,1)}), bf16[1024,4096]{1,0:T(8,128)(2,1)}) %all-gather.12.cloned.1.call-update) | async-done | bytes 8388624 | tf_op jit(solution)/shard_map/all_gather | solution.py:150
  710.8 11.2 %convolution_convert_fusion = bf16[512,4096]{1,0:T(8,128)(2,1)} fusion(bf16[1024,4096]{1,0:T(8,128)(2,1)} %all-gather.12.cloned.1.call-done, f32[2,512,1024]{2,1,0:T(8,128)} %fusion.29), kind=kOutput, calls=%fused_computation.21 | convolution fusion | flops 4300210176 | bytes 16777216 | tf_op jit(solution)/shard_map/dot_general | solution.py:148
  722.0 0.7 all-gather.14.cloned.1.call-update
  723.3 41.5 %reduce-scatter.3.cloned.1.call-done = bf16[512,1024]{1,0:T(8,128)(2,1)} async-done(((bf16[512,4096]{1,0:T(8,128)(2,1)}), bf16[512,1024]{1,0:T(8,128)(2,1)}) %reduce-scatter.3.cloned.1.call-update) | async-done | bytes 1048592 | tf_op jit(solution)/shard_map/reduce_scatter | solution.py:153
  764.8 2.0 add_convert_fusion
  766.8 2.1 gather_fusion.1
  768.8 0.7 reshape.383
  770.0 1.0 multiply_reduce_fusion
  771.0 5.7 all-reduce
  776.8 217.8 %all-gather.14.cloned.1.call-done = bf16[4,1024,2048]{2,1,0:T(8,128)(2,1)} async-done(((bf16[4,1024,256]{2,1,0:T(8,128)(2,1)}), bf16[4,1024,2048]{2,1,0:T(8,128)(2,1)}) %all-gather.14.cloned.1.call-update) | async-done | bytes 16777232 | tf_op jit(solution)/shard_map/all_gather | solution.py:169
  994.6 10.1 fusion.28
  1005.7 0.6 gather_fusion
  1006.6 18.2 %reduce-scatter.5.cloned.1.call-done = bf16[128,512]{1,0:T(8,128)(2,1)} async-done(((bf16[128,2048]{1,0:T(8,128)(2,1)}), bf16[128,512]{1,0:T(8,128)(2,1)}) %reduce-scatter.5.cloned.1.call-update) | async-done | bytes 131088 | tf_op jit(solution)/shard_map/reduce_scatter | solution.py:175
  1024.8 2.1 scatter_custom_fusion
  1026.9 5.5 all-to-all-start
  1032.4 0.7 select_reduce_fusion.1
  1033.1 6.7 all-to-all-done
  1040.0 5.9 psum.31
  1045.9 0.5 add_sqrt_fusion
  1046.4 0.7 copy.66
  (74 shorter events, 3.5 us)
Async XLA Ops:
  7.2 997.6 %copy-start = (s32[1024,1]{0,1:T(1,128)S(1)}, s32[1024,1]{0,1:T(1,128)}, u32[]{:S(2)}) copy-start(s32[1024,1]{0,1:T(1,128)} %param.19) | copy-start | bytes 12292
  7.2 182.2 %all-gather.6.cloned.1.call-start = ((), (), s32[]{:S(2)}) async-start(), calls=%async_computation.3 | async-start | bytes 14155776 | tf_op jit(solution)/shard_map/all_gather | solution.py:119
  7.9 256.7 %all-gather.8.cloned.1.call-start = ((), (), s32[]{:S(2)}) async-start(), calls=%async_computation.4 | async-start | bytes 4718592 | tf_op jit(solution)/shard_map/all_gather | solution.py:131
  8.7 346.4 %all-reduce.3.cloned.1.call-start = ((), (), s32[]{:S(2)}) async-start(), calls=%async_computation.5 | async-start | bytes 8388608 | tf_op jit(solution)/shard_map/psum | solution.py:134
  8.7 5.6 copy-start.2
  11.4 7.5 copy-start.11
  11.4 7.5 copy-start.12
  201.0 1.7 copy-start.8
  203.4 2.2 copy-start.4
  203.4 2.2 copy-start.5
  203.4 2.2 copy-start.6
  203.4 2.2 copy-start.7
  271.2 1.5 copy-start.13
  271.2 313.9 %all-gather.10.cloned.1.call-start = ((), (), s32[]{:S(2)}) async-start(), calls=%async_computation.6 | async-start | bytes 18874368 | tf_op jit(solution)/shard_map/all_gather | solution.py:144
  271.8 439.0 %all-gather.12.cloned.1.call-start = ((), (), s32[]{:S(2)}) async-start(), calls=%async_computation.7 | async-start | bytes 9437184 | tf_op jit(solution)/shard_map/all_gather | solution.py:150
  272.4 492.4 %reduce-scatter.3.cloned.1.call-start = ((), (), s32[]{:S(2)}) async-start(), calls=%async_computation.8 | async-start | bytes 5242880 | tf_op jit(solution)/shard_map/reduce_scatter | solution.py:153
  360.6 1.9 copy-start.3
  721.9 1.1 copy-start.14
  721.9 272.7 %all-gather.14.cloned.1.call-start = ((), (), s32[]{:S(2)}) async-start(), calls=%async_computation.9 | async-start | bytes 18874368 | tf_op jit(solution)/shard_map/all_gather | solution.py:169
  722.7 302.1 %reduce-scatter.5.cloned.1.call-start = ((), (), s32[]{:S(2)}) async-start(), calls=%async_computation.10 | async-start | bytes 655360 | tf_op jit(solution)/shard_map/reduce_scatter | solution.py:175
  768.8 225.8 %copy-start.9 = (f32[4,1024]{1,0:T(4,128)S(1)}, f32[4,1024]{1,0:T(4,128)}, u32[]{:S(2)}) copy-start(f32[4,1024]{1,0:T(4,128)} %param.28) | copy-start | bytes 49156
  768.8 225.8 %copy-start.10 = (f32[4,1024]{1,0:T(4,128)S(1)}, f32[4,1024]{1,0:T(4,128)}, u32[]{:S(2)}) copy-start(f32[4,1024]{1,0:T(4,128)} %param.27) | copy-start | bytes 49156
  994.6 11.0 %copy-start.1 = (s32[2,2]{1,0:T(2,128)S(1)}, s32[2,2]{1,0:T(2,128)}, u32[]{:S(2)}) copy-start(s32[2,2]{1,0:T(2,128)} %param.16) | copy-start | bytes 52
  1026.9 12.9 %all-to-all-start = ((bf16[8,16,512]{2,1,0:T(8,128)(2,1)}), bf16[8,16,512]{2,1,0:T(8,128)(2,1)S(1)}, u32[]{:S(2)}, u32[]{:S(2)}) async-start(bf16[8,16,512]{2,1,0:T(8,128)(2,1)} %bitcast.18), calls=%async_computation.2 | async-start | bytes 262144 | tf_op jit(solution)/shard_map/all_to_all | solution.py:192
Sparse Core Ops, SparseCore 0:
  10.2 179.1 all-gather.5
  191.4 73.1 all-gather.7
  271.3 83.6 all-reduce.2
  357.3 227.7 all-gather.9
  587.1 123.5 all-gather.11
  722.1 42.6 reduce-scatter.2
  766.8 227.7 all-gather.13
  1004.9 19.8 reduce-scatter.4
where the time goes:
time: 1050 us
  waiting for transfers between devices  925 us (88%)
  matrix products  59.2 us (6%)
  other arithmetic  27.4 us (3%)
  between operations  14.5 us (1%)
  blocking collectives  11.6 us (1%)
    all_gather x1, waiting for transfers between devices, on_device(): lax.all_gather(gate_up, 'req', axis=1, tiled=True)  221 us
    all_gather x1, waiting for transfers between devices, on_device(): piece_rows = lax.all_gather(merge_weight, 'req', axis=2, tiled=True)  218 us
    all_gather x1, waiting for transfers between devices, on_device(): lax.all_gather(qkv_weight, 'req', axis=0, tiled=True)  170 us
    all_gather x1, waiting for transfers between devices, on_device(): lax.all_gather(down_weight, 'req', axis=1, tiled=True)  111 us
    psum x1, waiting for transfers between devices, on_device(): lax.psum(head_terms.astype(jnp.bfloat16), 'mlp').astype(jnp.float32)  82.3 us
    all_gather x1, waiting for transfers between devices, on_device(): lax.all_gather(out_weight, 'req', axis=1, tiled=True)  52.4 us
    reduce_scatter x1, waiting for transfers between devices, on_device(): lax.psum_scatter(hidden_terms.astype(jnp.bfloat16), 'mlp', scatter_dimens...  41.5 us
  transfers between devices with their start and end apart: 9, of which 9 were waited for; matrix products, arithmetic and copies ran while one was open for 6% of the time, Pallas kernels for 0%

commit v1 on v0

--- a/solution.py
+++ b/solution.py
@@ -138,12 +138,27 @@
         jnp.bfloat16
     )
     columns = normed_two
-    gate_pair = jnp.einsum(
+    length, mine = (lax.axis_size("req"), lax.axis_index("req"))
+    left = [(i, (i - 1) % length) for i in range(length)]
+    extent = gate_up.shape[1]
+    held = gate_up
+    total = jnp.einsum(
         "rk,pkn->prn",
-        columns,
-        lax.all_gather(gate_up, "req", axis=1, tiled=True),
-        preferred_element_type=jnp.float32,
-    )
+        lax.dynamic_slice_in_dim(columns, mine * extent, held.shape[1], axis=1),
+        held,
+        preferred_element_type=jnp.float32,
+    )
+    for lap in range(1, length):
+        held = lax.ppermute(held, "req", left)
+        total = total + jnp.einsum(
+            "rk,pkn->prn",
+            lax.dynamic_slice_in_dim(
+                columns, (mine + lap) % length * extent, held.shape[1], axis=1
+            ),
+            held,
+            preferred_element_type=jnp.float32,
+        )
+    gate_pair = total
     hidden = (jax.nn.silu(gate_pair[0]) * gate_pair[1]).astype(jnp.bfloat16)
     hidden_terms = jnp.dot(
         hidden,

time: 1050 us -> 1040 us (level)
  waiting for transfers between devices: 925 us -> 857 us
  starting transfers between devices: 6.32 us -> 38.9 us
  matrix products: 59.2 us -> 74.9 us
    ppermute x0 -> x7, waiting for transfers between devices: none -> 354 us  [on_device(): held = lax.ppermute(held, 'req', left)]
    all_gather x1 -> x0, waiting for transfers between devices: 221 us -> none  [on_device(): lax.all_gather(gate_up, 'req', axis=1, tiled=True)]
    all_gather x1, waiting for transfers between devices: 111 us -> 0.01 us  [on_device(): lax.all_gather(down_weight, 'req', axis=1, tiled=True)]
    psum x1, waiting for transfers between devices: 82.3 us -> 0.01 us  [on_device(): lax.psum(head_terms.astype(jnp.bfloat16), 'mlp').astype(jnp.float32)]
    ppermute x0 -> x7, starting transfers between devices: none -> 32.9 us  [on_device(): held = lax.ppermute(held, 'req', left)]
    dot_general x1 -> x8, matrix products: 15 us -> 30.4 us  [the longest x7 29.2 us: on_device(): jnp.einsum('rk,pkn->prn', lax.dynamic_slice_in_dim(columns, (mine + lap)...]
    all_gather x1, waiting for transfers between devices: 170 us -> 158 us  [on_device(): lax.all_gather(qkv_weight, 'req', axis=0, tiled=True)]
  transfers between devices with their start and end apart: 9 -> 15, of which waited for: 9 -> 12; matrix products, arithmetic and copies ran while one was open for 6% -> 8% of each run, Pallas kernels for 0% -> 0%
where the time goes in v1:
time: 1040 us
  waiting for transfers between devices  857 us (82%)
  matrix products  74.9 us (7%)
  starting transfers between devices  38.9 us (4%)
  other arithmetic  28.6 us (3%)
  between operations  14.9 us (1%)
  blocking collectives  11.7 us (1%)
  local copies, waits for them, and re-layouts  11.4 us (1%)
    ppermute x7, waiting for transfers between devices, on_device(): held = lax.ppermute(held, 'req', left)  354 us
    all_gather x1, waiting for transfers between devices, on_device(): piece_rows = lax.all_gather(merge_weight, 'req', axis=2, tiled=True)  218 us
    all_gather x1, waiting for transfers between devices, on_device(): lax.all_gather(qkv_weight, 'req', axis=0, tiled=True)  158 us
    all_gather x1, waiting for transfers between devices, on_device(): lax.all_gather(out_weight, 'req', axis=1, tiled=True)  55.5 us
    reduce_scatter x1, waiting for transfers between devices, on_device(): lax.psum_scatter(hidden_terms.astype(jnp.bfloat16), 'mlp', scatter_dimens...  45.6 us
    ppermute x7, starting transfers between devices, on_device(): held = lax.ppermute(held, 'req', left)  32.9 us
    dot_general x7, matrix products, on_device(): jnp.einsum('rk,pkn->prn', lax.dynamic_slice_in_dim(columns, (mine + lap)...  29.2 us
  transfers between devices with their start and end apart: 15, of which 12 were waited for; matrix products, arithmetic and copies ran while one was open for 8% of the time, Pallas kernels for 0%

profile of v1, /device:TPU:0, one launch (start us, length us, event | category | flops | bytes accessed | tf_op | source)
XLA Modules:
  0.0 1037.5 jit_solution(666846459537921218)
XLA Ops:
  8.0 6.0 collective-permute-start
  15.2 3.0 convert_reduce_fusion
  18.2 1.2 fusion.4
  20.0 3.0 multiply_cosine_fusion.1
  23.1 73.2 %collective-permute-done = bf16[2,512,1024]{2,1,0:T(8,128)(2,1)} collective-permute-done((bf16[2,512,1024]{2,1,0:T(8,128)(2,1)}, bf16[2,512,1024]{2,1,0:T(8,128)(2,1)}, u32[]{:S(2)}, u32[]{:S(2)}) %collective-permute-start) | collective-permute-done | bytes 2097184 | tf_op jit(solution)/shard_map/ppermute | solution.py:152
  96.3 5.2 collective-permute-start.1
  101.5 157.9 %all-gather.5.cloned.1.call-done = bf16[4096,1536]{1,0:T(8,128)(2,1)} async-done(((bf16[512,1536]{1,0:T(8,128)(2,1)}), bf16[4096,1536]{1,0:T(8,128)(2,1)}) %all-gather.5.cloned.1.call-update) | async-done | bytes 12582928 | tf_op jit(solution)/shard_map/all_gather | solution.py:119
  259.4 11.8 %fusion.13 = f32[512,1536]{0,1:T(8,128)S(1)} fusion(bf16[4096,1536]{1,0:T(8,128)(2,1)} %all-gather.5.cloned.1.call-done, bf16[512,4096]{1,0:T(8,128)(2,1)} %param.15, f32[4096]{0:T(1024)S(1)} %bitcast.86, f32[4096]{0:T(1024)S(1)} %bitcast.85, f32[512]{0:T(512)S(1)} %add_rsqrt_fusion.1, f32[512]{0:T(512)S(1)} %broadcast_multiply_fusion.1), kind=kOutput, calls=%fused_computation.23 | convolution fusion | flops 6455033856 | bytes 19959808 | tf_op jit(solution)/shard_map/dot_general | solution.py:117
  271.4 1.5 copy-done.12
  273.6 2.2 subtract_convert_fusion.1
  276.7 2.1 fusion.19
  279.7 2.7 fusion.29
  282.4 55.5 %all-gather.7.cloned.1.call-done = bf16[512,4096]{1,0:T(8,128)(2,1)} async-done(((bf16[512,512]{1,0:T(8,128)(2,1)}), bf16[512,4096]{1,0:T(8,128)(2,1)}) %all-gather.7.cloned.1.call-update) | async-done | bytes 4194320 | tf_op jit(solution)/shard_map/all_gather | solution.py:131
  337.9 6.6 convolution_convert_fusion.1
  344.5 1.5 collective-permute-start.2
  346.1 46.0 %collective-permute-done.2 = bf16[2,512,1024]{2,1,0:T(8,128)(2,1)S(1)} collective-permute-done((bf16[2,512,1024]{2,1,0:T(8,128)(2,1)}, bf16[2,512,1024]{2,1,0:T(8,128)(2,1)S(1)}, u32[]{:S(2)}, u32[]{:S(2)}) %collective-permute-start.2) | collective-permute-done | bytes 2097184 | tf_op jit(solution)/shard_map/ppermute | solution.py:152
  392.1 4.3 collective-permute-start.3
  396.4 45.3 %collective-permute-done.3 = bf16[2,512,1024]{2,1,0:T(8,128)(2,1)S(1)} collective-permute-done((bf16[2,512,1024]{2,1,0:T(8,128)(2,1)S(1)}, bf16[2,512,1024]{2,1,0:T(8,128)(2,1)S(1)}, u32[]{:S(2)}, u32[]{:S(2)}) %collective-permute-start.3) | collective-permute-done | bytes 2097184 | tf_op jit(solution)/shard_map/ppermute | solution.py:152
  441.8 1.3 copy-done.10
  443.1 5.3 collective-permute-start.4
  448.4 71.0 %collective-permute-done.4 = bf16[2,512,1024]{2,1,0:T(8,128)(2,1)} collective-permute-done((bf16[2,512,1024]{2,1,0:T(8,128)(2,1)S(1)}, bf16[2,512,1024]{2,1,0:T(8,128)(2,1)}, u32[]{:S(2)}, u32[]{:S(2)}) %collective-permute-start.4) | collective-permute-done | bytes 2097184 | tf_op jit(solution)/shard_map/ppermute | solution.py:152
  519.3 5.3 collective-permute-start.5
  524.7 88.6 %collective-permute-done.5 = bf16[2,512,1024]{2,1,0:T(8,128)(2,1)} collective-permute-done((bf16[2,512,1024]{2,1,0:T(8,128)(2,1)}, bf16[2,512,1024]{2,1,0:T(8,128)(2,1)}, u32[]{:S(2)}, u32[]{:S(2)}) %collective-permute-start.5) | collective-permute-done | bytes 2097184 | tf_op jit(solution)/shard_map/ppermute | solution.py:152
  613.3 5.2 collective-permute-start.6
  618.5 5.6 convert_reduce_fusion.1
  625.4 2.4 fusion.11
  627.9 1.3 fusion.67
  629.1 1.8 copy-done.11
  630.9 1.3 fusion.59
  632.2 1.3 fusion.61
  633.5 2.9 fusion.63
  636.4 4.8 fusion.57
  641.2 4.8 fusion.65
  646.0 4.8 fusion.55
  650.8 30.3 %collective-permute-done.6 = bf16[2,512,1024]{2,1,0:T(8,128)(2,1)} collective-permute-done((bf16[2,512,1024]{2,1,0:T(8,128)(2,1)}, bf16[2,512,1024]{2,1,0:T(8,128)(2,1)}, u32[]{:S(2)}, u32[]{:S(2)}) %collective-permute-start.6) | collective-permute-done | bytes 2097184 | tf_op jit(solution)/shard_map/ppermute | solution.py:152
  681.2 9.3 add_bitcast_fusion
  690.5 11.2 %convolution_convert_fusion = bf16[512,4096]{1,0:T(8,128)(2,1)} fusion(bf16[1024,4096]{1,0:T(8,128)(2,1)} %all-gather.9.cloned.1.call-done, f32[2,512,1024]{2,1,0:T(8,128)} %add_bitcast_fusion), kind=kOutput, calls=%fused_computation.21 | convolution fusion | flops 4300210176 | bytes 16777216 | tf_op jit(solution)/shard_map/dot_general | solution.py:163
  702.8 45.6 %reduce-scatter.3.cloned.1.call-done = bf16[512,1024]{1,0:T(8,128)(2,1)} async-done(((bf16[512,4096]{1,0:T(8,128)(2,1)}), bf16[512,1024]{1,0:T(8,128)(2,1)}) %reduce-scatter.3.cloned.1.call-update) | async-done | bytes 1048592 | tf_op jit(solution)/shard_map/reduce_scatter | solution.py:168
  748.3 2.0 add_convert_fusion
  750.3 2.1 gather_fusion.1
  754.6 5.7 all-reduce
  760.3 217.7 %all-gather.11.cloned.1.call-done = bf16[4,1024,2048]{2,1,0:T(8,128)(2,1)} async-done(((bf16[4,1024,256]{2,1,0:T(8,128)(2,1)}), bf16[4,1024,2048]{2,1,0:T(8,128)(2,1)}) %all-gather.11.cloned.1.call-update) | async-done | bytes 16777232 | tf_op jit(solution)/shard_map/all_gather | solution.py:184
  978.0 10.1 fusion.21
  990.0 18.2 %reduce-scatter.5.cloned.1.call-done = bf16[128,512]{1,0:T(8,128)(2,1)} async-done(((bf16[128,2048]{1,0:T(8,128)(2,1)}), bf16[128,512]{1,0:T(8,128)(2,1)}) %reduce-scatter.5.cloned.1.call-update) | async-done | bytes 131088 | tf_op jit(solution)/shard_map/reduce_scatter | solution.py:190
  1008.2 2.1 scatter_custom_fusion
  1010.3 5.5 all-to-all-start
  1016.5 6.7 all-to-all-done
  1023.3 5.9 psum.31
  (103 shorter events, 13.6 us)
Async XLA Ops:
  7.2 981.0 %copy-start = (s32[1024,1]{0,1:T(1,128)S(1)}, s32[1024,1]{0,1:T(1,128)}, u32[]{:S(2)}) copy-start(s32[1024,1]{0,1:T(1,128)} %param.19) | copy-start | bytes 12292
  7.2 252.2 %all-gather.5.cloned.1.call-start = ((), (), s32[]{:S(2)}) async-start(), calls=%async_computation.3 | async-start | bytes 14155776 | tf_op jit(solution)/shard_map/all_gather | solution.py:119
  7.9 330.0 %all-gather.7.cloned.1.call-start = ((), (), s32[]{:S(2)}) async-start(), calls=%async_computation.4 | async-start | bytes 4718592 | tf_op jit(solution)/shard_map/all_gather | solution.py:131
  8.0 88.3 %collective-permute-start = (bf16[2,512,1024]{2,1,0:T(8,128)(2,1)}, bf16[2,512,1024]{2,1,0:T(8,128)(2,1)}, u32[]{:S(2)}, u32[]{:S(2)}) collective-permute-start(bf16[2,512,1024]{2,1,0:T(8,128)(2,1)} %param.25), channel_id=1, source_target_pairs={{0,28},{4,0},{8,4},{12,8},{16,12},{20,16},{24,20},{28,24},{1,29},{... | collective-permute-start | bytes 6291464 | tf_op jit(solution)/shard_map/ppermute | solution.py:152
  14.0 604.5 %all-reduce.3.cloned.1.call-start = ((), (), s32[]{:S(2)}) async-start(), calls=%async_computation.5 | async-start | bytes 8388608 | tf_op jit(solution)/shard_map/psum | solution.py:134
  14.1 4.2 copy-start.3
  15.1 4.3 copy-start.19
  15.1 7.9 copy-start.15
  15.2 7.9 copy-start.16
  96.3 248.2 %collective-permute-start.1 = (bf16[2,512,1024]{2,1,0:T(8,128)(2,1)}, bf16[2,512,1024]{2,1,0:T(8,128)(2,1)}, u32[]{:S(2)}, u32[]{:S(2)}) collective-permute-start(bf16[2,512,1024]{2,1,0:T(8,128)(2,1)} %collective-permute-done), channel_id=1, source_target_pairs={{0,28},{4,0},{8,4},{12,8},{16,12},{20,16},{24,20},{28,24},{1,29},{... | collective-permute-start | bytes 6291464 | tf_op jit(solution)/shard_map/ppermute | solution.py:152
  271.2 1.7 copy-start.12
  273.6 2.2 copy-start.5
  273.6 2.2 copy-start.6
  273.6 2.2 copy-start.7
  273.6 2.2 copy-start.8
  344.4 180.2 %copy-start.17 = (f32[2,4096]{1,0:T(2,128)S(1)}, f32[2,4096]{1,0:T(2,128)}, u32[]{:S(2)}) copy-start(f32[2,4096]{1,0:T(2,128)} %param.22) | copy-start | bytes 98308
  344.5 346.0 %all-gather.9.cloned.1.call-start = ((), (), s32[]{:S(2)}) async-start(), calls=%async_computation.6 | async-start | bytes 9437184 | tf_op jit(solution)/shard_map/all_gather | solution.py:165
  344.5 47.6 %collective-permute-start.2 = (bf16[2,512,1024]{2,1,0:T(8,128)(2,1)}, bf16[2,512,1024]{2,1,0:T(8,128)(2,1)S(1)}, u32[]{:S(2)}, u32[]{:S(2)}) collective-permute-start(bf16[2,512,1024]{2,1,0:T(8,128)(2,1)} %collective-permute-done.1), channel_id=1, source_target_pairs={{0,28},{4,0},{8,4},{12,8},{16,12},{20,16},{24,20},{28,24},{1,29},{... | collective-permute-start | bytes 6291464 | tf_op jit(solution)/shard_map/ppermute | solution.py:152
  346.0 402.3 %reduce-scatter.3.cloned.1.call-start = ((), (), s32[]{:S(2)}) async-start(), calls=%async_computation.7 | async-start | bytes 5242880 | tf_op jit(solution)/shard_map/reduce_scatter | solution.py:168
  392.1 49.7 %collective-permute-start.3 = (bf16[2,512,1024]{2,1,0:T(8,128)(2,1)S(1)}, bf16[2,512,1024]{2,1,0:T(8,128)(2,1)S(1)}, u32[]{:S(2)}, u32[]{:S(2)}) collective-permute-start(bf16[2,512,1024]{2,1,0:T(8,128)(2,1)S(1)} %collective-permute-done.2), channel_id=1, source_target_pairs={{0,28},{4,0},{8,4},{12,8},{16,12},{20,16},{24,20},{28,24},{1,29},{... | collective-permute-start | bytes 6291464 | tf_op jit(solution)/shard_map/ppermute | solution.py:152
  441.8 1.3 copy-start.10
  443.1 76.2 %collective-permute-start.4 = (bf16[2,512,1024]{2,1,0:T(8,128)(2,1)S(1)}, bf16[2,512,1024]{2,1,0:T(8,128)(2,1)}, u32[]{:S(2)}, u32[]{:S(2)}) collective-permute-start(bf16[2,512,1024]{2,1,0:T(8,128)(2,1)S(1)} %collective-permute-done.3), channel_id=1, source_target_pairs={{0,28},{4,0},{8,4},{12,8},{16,12},{20,16},{24,20},{28,24},{1,29},{... | collective-permute-start | bytes 6291464 | tf_op jit(solution)/shard_map/ppermute | solution.py:152
  519.3 94.0 %collective-permute-start.5 = (bf16[2,512,1024]{2,1,0:T(8,128)(2,1)}, bf16[2,512,1024]{2,1,0:T(8,128)(2,1)}, u32[]{:S(2)}, u32[]{:S(2)}) collective-permute-start(bf16[2,512,1024]{2,1,0:T(8,128)(2,1)} %collective-permute-done.4), channel_id=1, source_target_pairs={{0,28},{4,0},{8,4},{12,8},{16,12},{20,16},{24,20},{28,24},{1,29},{... | collective-permute-start | bytes 6291464 | tf_op jit(solution)/shard_map/ppermute | solution.py:152
  613.3 67.9 %collective-permute-start.6 = (bf16[2,512,1024]{2,1,0:T(8,128)(2,1)}, bf16[2,512,1024]{2,1,0:T(8,128)(2,1)}, u32[]{:S(2)}, u32[]{:S(2)}) collective-permute-start(bf16[2,512,1024]{2,1,0:T(8,128)(2,1)} %collective-permute-done.5), channel_id=1, source_target_pairs={{0,28},{4,0},{8,4},{12,8},{16,12},{20,16},{24,20},{28,24},{1,29},{... | collective-permute-start | bytes 6291464 | tf_op jit(solution)/shard_map/ppermute | solution.py:152
  624.1 3.7 copy-start.2
  625.4 2.5 copy-start.9
  627.8 18.2 %copy-start.4 = (bf16[512,4096]{1,0:T(8,128)(2,1)}, bf16[512,4096]{1,0:T(8,128)(2,1)S(1)}, u32[]{:S(2)}) copy-start(bf16[512,4096]{1,0:T(8,128)(2,1)S(1)} %fusion.11) | copy-start | bytes 12582916
  627.8 3.1 copy-start.11
  701.6 0.9 copy-start.18
  701.7 276.4 %all-gather.11.cloned.1.call-start = ((), (), s32[]{:S(2)}) async-start(), calls=%async_computation.8 | async-start | bytes 18874368 | tf_op jit(solution)/shard_map/all_gather | solution.py:184
  702.2 306.0 %reduce-scatter.5.cloned.1.call-start = ((), (), s32[]{:S(2)}) async-start(), calls=%async_computation.9 | async-start | bytes 655360 | tf_op jit(solution)/shard_map/reduce_scatter | solution.py:190
  752.4 225.7 %copy-start.13 = (f32[4,1024]{1,0:T(4,128)S(1)}, f32[4,1024]{1,0:T(4,128)}, u32[]{:S(2)}) copy-start(f32[4,1024]{1,0:T(4,128)} %param.28) | copy-start | bytes 49156
  752.4 225.7 %copy-start.14 = (f32[4,1024]{1,0:T(4,128)S(1)}, f32[4,1024]{1,0:T(4,128)}, u32[]{:S(2)}) copy-start(f32[4,1024]{1,0:T(4,128)} %param.27) | copy-start | bytes 49156
  978.0 11.0 %copy-start.1 = (s32[2,2]{1,0:T(2,128)S(1)}, s32[2,2]{1,0:T(2,128)}, u32[]{:S(2)}) copy-start(s32[2,2]{1,0:T(2,128)} %param.16) | copy-start | bytes 52
  1010.3 12.8 %all-to-all-start = ((bf16[8,16,512]{2,1,0:T(8,128)(2,1)}), bf16[8,16,512]{2,1,0:T(8,128)(2,1)S(1)}, u32[]{:S(2)}, u32[]{:S(2)}) async-start(bf16[8,16,512]{2,1,0:T(8,128)(2,1)} %bitcast.25), calls=%async_computation.2 | async-start | bytes 262144 | tf_op jit(solution)/shard_map/all_to_all | solution.py:207
Sparse Core Ops, SparseCore 0:
  10.2 249.1 all-gather.4
  261.4 76.4 all-gather.6
  344.6 83.6 all-reduce.2
  430.4 227.3 all-gather.8
  701.8 46.5 reduce-scatter.2
  750.2 227.7 all-gather.10
  988.3 19.8 reduce-scatter.4
